TPU v7x, 512 devices: a whole 4x8x8 slice. The times are simulated.
512 devices in a mesh: ctx: 64 (over x, y, core), kvh: 8 (over z).
Axes of the slice: x: 4, y: 8, z: 8, core: 2. Of those that a mesh axis runs over, the one named last changes fastest.
Arguments:
- ctx_q: bfloat16 [8192, 8192], P('ctx', 'kvh'), may hold values from -160 to 160
- ctx_kv: bfloat16 [2, 8192, 1024], P(None, 'ctx', 'kvh'), may hold values from -6 to 6
- quest_q: bfloat16 [64, 128, 8192], P('ctx', None, 'kvh'), may hold values from -160 to 160
- quest_kv: bfloat16 [64, 2, 128, 1024], P('ctx', None, None, 'kvh'), may hold values from -6 to 6
- quest_len: int32 [1], replicated, may hold values from 64 to 128
- host_block: int32 [1], replicated, may hold values from 1 to 63
- out_weight: bfloat16 [8192, 8192], P('kvh', 'ctx'), may hold values from -0.0625 to 0.0625
Outputs:
- ctx_out: bfloat16 [8192, 8192], P('ctx', 'kvh')
- quest_out: bfloat16 [128, 8192], P('kvh', 'ctx')
All inputs are finite; a program needn't handle non-finite values.
Results may differ from a plain program's by a relative error of at most 0.019.
Values may be sent and summed in bfloat16 or wider, within the bound.
A program may use at most 192 MiB of HBM per device.

v0:
```python
import jax
import jax.numpy as jnp
from jax import lax
from jax.sharding import PartitionSpec as P

DH = 128


MASKED = -1e30


def from_root(block, axis, owner):
    block = jnp.where(lax.axis_index(axis) == owner, block, jnp.zeros_like(block))
    return lax.psum(block, axis)


def head_scores(queries, key_rows, visible):
    scores = jnp.dot(queries, key_rows.T, preferred_element_type=jnp.float32) * DH ** (-0.5)
    return jnp.where(visible, scores, MASKED)


def attend_heads(queries, key_rows, val_rows, visible):
    heads = queries.shape[1] // DH
    output = jnp.zeros(queries.shape, jnp.bfloat16)

    def attend_loop_body(head_idx, output):
        query_head = lax.dynamic_slice_in_dim(queries, head_idx * DH, DH, 1)
        scores = head_scores(query_head, key_rows, visible)
        maximum = jnp.max(scores, axis=1, keepdims=True)
        weights = jnp.exp(scores - maximum)
        totals = jnp.sum(weights, axis=1, keepdims=True)
        numer = jnp.dot(weights.astype(jnp.bfloat16), val_rows, preferred_element_type=jnp.float32)
        return lax.dynamic_update_slice_in_dim(
            output, (numer / totals).astype(jnp.bfloat16), head_idx * DH, 1
        )

    return lax.fori_loop(0, heads, attend_loop_body, output)


def partial_heads(queries, key_rows, val_rows, visible):
    heads = queries.shape[1] // DH
    rows_n = queries.shape[0]
    start_state = (
        jnp.zeros((rows_n, heads), jnp.float32),
        jnp.zeros((rows_n, heads), jnp.float32),
        jnp.zeros((rows_n, heads * DH), jnp.float32),
    )

    def partial_loop_body(head_idx, state):
        maxima, totals, numers = state
        query_head = lax.dynamic_slice_in_dim(queries, head_idx * DH, DH, 1)
        scores = head_scores(query_head, key_rows, visible)
        maximum = jnp.max(scores, axis=1)
        weights = jnp.exp(scores - maximum[:, None])
        total = jnp.sum(weights, axis=1)
        numer = jnp.dot(weights.astype(jnp.bfloat16), val_rows, preferred_element_type=jnp.float32)
        maxima = lax.dynamic_update_slice_in_dim(maxima, maximum[:, None], head_idx, 1)
        totals = lax.dynamic_update_slice_in_dim(totals, total[:, None], head_idx, 1)
        numers = lax.dynamic_update_slice_in_dim(numers, numer, head_idx * DH, 1)
        return (maxima, totals, numers)

    return lax.fori_loop(0, heads, partial_loop_body, start_state)


def combine_states(first, second):
    max_a, tot_a, num_a = first
    max_b, tot_b, num_b = second
    joined = jnp.maximum(max_a, max_b)
    fac_a = jnp.exp(max_a - joined)
    fac_b = jnp.exp(max_b - joined)
    width = num_a.shape[1] // max_a.shape[1]
    numers = num_a * jnp.repeat(fac_a, width, axis=1) + num_b * jnp.repeat(fac_b, width, axis=1)
    return (joined, tot_a * fac_a + tot_b * fac_b, numers)


def finish_rows(numers, totals, row_ids, length):
    attn = numers / jnp.repeat(totals, DH, axis=1)
    return jnp.where(row_ids[:, None] < length, attn, 0.0).astype(jnp.bfloat16)


def per_device(ctx_q, ctx_kv, quest_q, quest_kv, quest_len, host_block, out_weight):
    blk_rows = ctx_q.shape[0]
    block = lax.axis_index("ctx")
    anchor_kv = from_root(ctx_kv, "ctx", 0)
    key_rows = jnp.concatenate([anchor_kv[0], ctx_kv[0]], axis=0)
    val_rows = jnp.concatenate([anchor_kv[1], ctx_kv[1]], axis=0)
    row_ids = jnp.arange(blk_rows, dtype=jnp.int32)[:, None]
    col_ids = jnp.arange(2 * blk_rows, dtype=jnp.int32)[None, :]
    visible = jnp.where(col_ids < blk_rows, block > 0, col_ids - blk_rows <= row_ids)
    ctx_out = attend_heads(ctx_q, key_rows, val_rows, visible)
    length = quest_len[0]
    host = host_block[0]
    question = from_root(quest_q, "ctx", host)[0]
    slots = question.shape[0]
    all_visible = jnp.ones((slots, blk_rows), dtype=bool)
    ctx_state = partial_heads(question, ctx_kv[0], ctx_kv[1], all_visible)
    q_rows = jnp.arange(slots, dtype=jnp.int32)[:, None]
    q_cols = jnp.arange(slots, dtype=jnp.int32)[None, :]
    own_visible = (q_cols <= q_rows) & (q_cols < length)
    own_max, own_tot, own_num = partial_heads(question, quest_kv[0, 0], quest_kv[0, 1], own_visible)
    is_host = block == host
    own_state = (
        jnp.where(is_host, own_max, MASKED),
        jnp.where(is_host, own_tot, 0.0),
        jnp.where(is_host, own_num, 0.0),
    )
    maxima, totals, numers = combine_states(ctx_state, own_state)
    all_rows = jnp.arange(slots, dtype=jnp.int32)
    overall = lax.pmax(maxima, "ctx")
    factor = jnp.exp(maxima - overall)
    sum_tot, sum_num = lax.psum((totals * factor, numers * jnp.repeat(factor, DH, axis=1)), "ctx")
    attn = finish_rows(sum_num, sum_tot, all_rows, length)
    quest_out = lax.psum_scatter(
        jnp.dot(attn, out_weight, preferred_element_type=jnp.float32).astype(jnp.bfloat16),
        "kvh",
        scatter_dimension=0,
        tiled=True,
    )
    return (ctx_out, quest_out)


def solution(mesh):
    return jax.shard_map(
        per_device,
        mesh=mesh,
        in_specs=(
            P("ctx", "kvh"),
            P(None, "ctx", "kvh"),
            P("ctx", None, "kvh"),
            P("ctx", None, None, "kvh"),
            P(),
            P(),
            P("kvh", "ctx"),
        ),
        out_specs=(P("ctx", "kvh"), P("kvh", "ctx")),
        check_vma=False,
    )
```

profile of v0, /device:TPU:1, one launch (start us, length us, event | category | flops | bytes accessed | tf_op | source)
XLA Modules:
  0.0 584.6 jit_solution(16561835068431018210)
XLA Ops:
  7.9 0.7 select_bitcast_fusion
  8.8 0.6 broadcast_select_fusion
  9.5 0.8 copy-done.3
  10.9 195.4 %all-reduce.6.cloned.1.call-done = (bf16[2,128,128]{2,1,0:T(8,128)(2,1)}, bf16[128,1024]{1,0:T(8,128)(2,1)}) async-done(((bf16[2,128,128]{2,1,0:T(8,128)(2,1)}, bf16[128,1024]{1,0:T(8,128)(2,1)}), (bf16[2,128,128]{2,1,0:T(8,128)(2,1)}, bf16[128,1024]{1,0:T(8,128)(2,1)})) %all-reduce.6.cloned.1.call-update) | async-done | bytes 327696 | tf_op jit(solution)/shard_map/psum | solution.py:14
  206.4 10.2 %while.49 = (s32[]{:T(128)}, f32[128,8]{0,1:T(8,128)S(1)}, f32[128,8]{0,1:T(8,128)S(1)}, f32[128,1024]{1,0:T(8,128)S(1)}, bf16[128,1024]{1,0:T(8,128)(2,1)}, /*i...) while((s32[]{:T(128)}, f32[128,8]{0,1:T(8,128)S(1)}, ...), condition=%wide.region_9.10_spmd, body=%wide.region_6.9_spmd.sunk | while | flops 8486662 | bytes 364715 | solution.py:62
  206.5 0.9 fusion.63
  207.4 0.2 convolution_dynamic-update-slice_fusion.4
  207.7 0.9 fusion.63
  208.7 0.2 convolution_dynamic-update-slice_fusion.4
  209.0 0.9 fusion.63
  209.9 0.2 convolution_dynamic-update-slice_fusion.4
  210.3 0.9 fusion.63
  211.2 0.2 convolution_dynamic-update-slice_fusion.4
  211.5 0.9 fusion.63
  212.5 0.2 convolution_dynamic-update-slice_fusion.4
  212.8 0.9 fusion.63
  213.7 0.2 convolution_dynamic-update-slice_fusion.4
  214.1 0.9 fusion.63
  215.0 0.2 convolution_dynamic-update-slice_fusion.4
  215.3 0.9 fusion.63
  216.3 0.2 convolution_dynamic-update-slice_fusion.4
  216.7 10.2 %while.51 = (s32[]{:T(128)}, f32[128,8]{0,1:T(8,128)S(1)}, f32[128,8]{0,1:T(8,128)S(1)}, f32[128,1024]{1,0:T(8,128)S(1)}, bf16[128,1024]{1,0:T(8,128)(2,1)}, /*i...) while((s32[]{:T(128)}, f32[128,8]{0,1:T(8,128)S(1)}, ...), condition=%wide.region_13.14_spmd.clone, body=%wide.region_10.13_spmd.clone.sunk | while | flops 8535814 | bytes 364851 | solution.py:62
  216.7 0.9 fusion.74
  217.6 0.2 convolution_dynamic-update-slice_fusion.5
  218.0 0.9 fusion.74
  218.9 0.2 convolution_dynamic-update-slice_fusion.5
  219.2 0.9 fusion.74
  220.2 0.2 convolution_dynamic-update-slice_fusion.5
  220.5 0.9 fusion.74
  221.4 0.2 convolution_dynamic-update-slice_fusion.5
  221.8 0.9 fusion.74
  222.7 0.2 convolution_dynamic-update-slice_fusion.5
  223.0 0.9 fusion.74
  224.0 0.2 convolution_dynamic-update-slice_fusion.5
  224.3 0.9 fusion.74
  225.2 0.2 convolution_dynamic-update-slice_fusion.5
  225.6 0.9 fusion.74
  226.5 0.2 convolution_dynamic-update-slice_fusion.5
  226.8 124.5 %pmax.7 = f32[128,8]{0,1:T(8,128)S(1)} all-reduce(f32[128,8]{0,1:T(8,128)S(1)} %select_maximum_fusion), channel_id=1, replica_groups=mesh['ctx'=64,'kvh'=8] {'ctx'}, use_global_device_ids=true, to_apply=%region_14.15 | all-reduce | flops 1024 | bytes 8192 | tf_op jit(solution)/shard_map/pmax | solution.py:109
  351.9 0.2 broadcast_in_dim.121
  352.1 0.2 broadcast_in_dim.122
  352.3 1.3 bitcast_multiply_fusion
  353.7 126.1 %psum.31 = f32[128,8]{0,1:T(8,128)S(1)} all-reduce(f32[128,8]{0,1:T(8,128)S(1)} %get-tuple-element.473), channel_id=1, replica_groups=mesh['ctx'=64,'kvh'=8] {'ctx'}, use_global_device_ids=true, to_apply=%region_16.17 | all-reduce | flops 1024 | bytes 8192 | tf_op jit(solution)/shard_map/psum | solution.py:111
  479.9 60.9 %all-reduce.4.cloned.1.call-done = f32[128,1024]{1,0:T(8,128)} async-done(((f32[128,1024]{1,0:T(8,128)}), f32[128,1024]{1,0:T(8,128)}) %all-reduce.4.cloned.1.call-update) | async-done | bytes 524304 | tf_op jit(solution)/shard_map/psum | solution.py:111
  541.0 0.8 copy-done.5
  541.9 0.9 convolution_convert_fusion
  542.8 11.8 %while.50 = (s32[]{:T(128)}, bf16[128,1024]{1,0:T(8,128)(2,1)S(1)}, bf16[128,1024]{1,0:T(8,128)(2,1)}, bf16[256,128]{1,0:T(8,128)(2,1)S(1)}, bf16[256,128]{1,0:T...) while((s32[]{:T(128)}, bf16[128,1024]{1,0:T(8,128)(2,1)S(1)}, ...), condition=%wide.region_4.5_spmd.clone, body=%wide.region_1.4_spmd.clone.sunk | while | flops 17104644 | bytes 594347 | solution.py:37
  542.8 1.0 fusion.68
  544.0 0.2 fusion.70
  544.3 1.0 fusion.68
  545.5 0.2 fusion.70
  545.8 1.0 fusion.68
  547.0 0.2 fusion.70
  547.2 1.0 fusion.68
  548.5 0.2 fusion.70
  548.7 1.0 fusion.68
  549.9 0.2 fusion.70
  550.2 1.0 fusion.68
  551.4 0.2 fusion.70
  551.7 1.0 fusion.68
  552.9 0.2 fusion.70
  553.1 1.0 fusion.68
  554.4 0.2 fusion.70
  554.6 23.5 %reduce-scatter.2.cloned.1.call-done = bf16[16,128]{1,0:T(8,128)(2,1)} async-done(((bf16[128,128]{1,0:T(8,128)(2,1)}), bf16[16,128]{1,0:T(8,128)(2,1)}) %reduce-scatter.2.cloned.1.call-update) | async-done | bytes 4112 | tf_op jit(solution)/shard_map/reduce_scatter | solution.py:113
  (94 shorter events, 4.5 us)
Async XLA Ops:
  7.2 533.8 %copy-start = (bf16[1024,128]{1,0:T(8,128)(2,1)S(1)}, bf16[1024,128]{1,0:T(8,128)(2,1)}, u32[]{:S(2)}) copy-start(bf16[1024,128]{1,0:T(8,128)(2,1)} %param.19) | copy-start | bytes 786436
  7.2 199.2 %all-reduce.6.cloned.1.call-start = ((), (), s32[]{:S(2)}) async-start(), calls=%async_computation.3 | async-start | bytes 655360 | tf_op jit(solution)/shard_map/psum | solution.py:14
  7.9 0.8 copy-start.2
  9.4 0.8 copy-start.3
  9.4 531.4 %all-reduce.4.cloned.1.call-start = ((), (), s32[]{:S(2)}) async-start(), calls=%async_computation.1 | async-start | bytes 1048576 | tf_op jit(solution)/shard_map/psum | solution.py:111
  353.6 126.2 %copy-start.4 = (bf16[2,128,128]{2,1,0:T(8,128)(2,1)S(1)}, bf16[2,128,128]{2,1,0:T(8,128)(2,1)}, u32[]{:S(2)}) copy-start(bf16[2,128,128]{2,1,0:T(8,128)(2,1)} %get-tuple-element.471) | copy-start | bytes 196612
  353.6 224.5 %reduce-scatter.2.cloned.1.call-start = ((), (), s32[]{:S(2)}) async-start(), calls=%async_computation.2 | async-start | bytes 36864 | tf_op jit(solution)/shard_map/reduce_scatter | solution.py:113
  540.8 1.0 copy-start.5
  554.6 23.5 %copy-start.1 = (bf16[128,1024]{1,0:T(8,128)(2,1)}, bf16[128,1024]{1,0:T(8,128)(2,1)S(1)}, u32[]{:S(2)}) copy-start(bf16[128,1024]{1,0:T(8,128)(2,1)S(1)} %get-tuple-element.376) | copy-start | bytes 786436
Sparse Core Ops, SparseCore 0:
  12.1 194.1 all-reduce.5
  353.7 187.0 all-reduce.3
  544.4 33.6 reduce-scatter.1
where the time goes:
time: 591 us; the launch traced here: 585 us
  waiting for transfers between devices  280 us (47%)
  blocking collectives  251 us (42%)
  matrix products  29.1 us (5%)
  between operations  15.3 us (3%)
    psum x1, waiting for transfers between devices, from_root(): return lax.psum(block, axis)  195 us
    psum x1, blocking collectives, per_device(): lax.psum((totals * factor, numers * jnp.repeat(factor, DH, axis=1)), 'ctx')  126 us
    pmax x1, blocking collectives, per_device(): overall = lax.pmax(maxima, 'ctx')  125 us
    psum x1, waiting for transfers between devices, per_device(): lax.psum((totals * factor, numers * jnp.repeat(factor, DH, axis=1)), 'ctx')  60.9 us
    reduce_scatter x1, waiting for transfers between devices, per_device(): lax.psum_scatter(jnp.dot(attn, out_weight, preferred_element_type=jnp.flo...  23.5 us
    dot_general x24, matrix products, head_scores(): jnp.dot(queries, key_rows.T, preferred_element_type=jnp.float32)  23.1 us
  transfers between devices with their start and end apart: 3, of which 3 were waited for; matrix products, arithmetic and copies ran while one was open for 2% of the time, Pallas kernels for 0%

commit v1 on v0

v1 whole, which is shorter than its diff:
```python
import math

import jax
import jax.numpy as jnp
from jax import lax
from jax.experimental import pallas as pl
from jax.experimental.pallas import tpu as pltpu
from jax.sharding import PartitionSpec as P


DH = 128
BLK = 128
HEADS = 8
HALF = 64
NX, NY, NZ = 4, 8, 8
GROUP = 16
NPG = 4
MASKED = -1e30
SCALE = DH ** (-0.5)
LOG2E = math.log2(math.e)
COEF = SCALE * LOG2E
MESH = pl.DeviceIdType.MESH


def dot_t(a, b):
    return lax.dot_general(a, b, (((1,), (1,)), ((), ())), preferred_element_type=jnp.float32)


def kernel(
    len_ref, host_ref, cq_hbm, ckv_hbm, qq_hbm, qkv_hbm, w_hbm,
    cout_hbm, qout_ref,
    cq, w, akv, kvall, q1buf, q1sel, q2buf, r1buf, r1sel, pbuf, lbuf, abuf, zsrc, zbuf, cout,
    lsem, osem, q1_s, q1_r, q2_s, q2_r, r1_s, r1_r, r2_s, r2_r, kv_s, kv_r, km_s, km_r,
    a1_s, a1_r, a2_s, a2_r, am_s, am_r, p_s, p_r, l_s, l_r, g_s, g_r, z_s, z_r,
):
    ctx = lax.axis_index("ctx")
    z = lax.axis_index("kvh")
    x = ctx // 16
    y = (ctx // 2) % NY
    c = ctx % 2
    yp = y % 2
    pg = y // 2
    head = x * 2 + c
    gid = c * 8 + x * 2 + yp

    def at(x2, y2, c2, z2):
        return ((x2 * NY + y2) * 2 + c2, z2)

    group = []
    for dx in range(NX):
        for dp in range(2):
            for dc in range(2):
                if dx or dp or dc:
                    x2 = (x + dx) % NX
                    yp2 = (yp + dp) % 2
                    c2 = (c + dc) % 2
                    group.append((dx, dp, dc, x2, yp2, c2, at(x2, pg * 2 + yp2, c2, z)))
    across = [at(x, (y + 2 * k) % NY, c, z) for k in range(1, NPG)]
    heads_z = [((z + k) % NZ, at(x, y, c, (z + k) % NZ)) for k in range(1, NZ)]
    mate = at(x, y, 1 - c, z)

    def local(src, dst, sem):
        cp = pltpu.make_async_copy(src, dst, sem)
        cp.start()
        return cp

    def send(src, dst, ssem, rsem, target):
        pltpu.make_async_remote_copy(
            src_ref=src, dst_ref=dst, send_sem=ssem, recv_sem=rsem, device_id=target, device_id_type=MESH
        ).start()

    def drain(ref, sem):
        pltpu.make_async_copy(ref, ref, sem).wait()

    load_q = local(cq_hbm, cq, lsem.at[0])
    load_own = local(ckv_hbm, akv.at[:, pl.ds(BLK, BLK), :], lsem.at[1])
    load_w = local(w_hbm, w, lsem.at[2])

    barrier = pltpu.get_barrier_semaphore()
    for member in group:
        pl.semaphore_signal(barrier, inc=1, device_id=member[-1], device_id_type=MESH)
    for target in across:
        pl.semaphore_signal(barrier, inc=1, device_id=target, device_id_type=MESH)
    for _, target in heads_z:
        pl.semaphore_signal(barrier, inc=1, device_id=target, device_id_type=MESH)
    pl.semaphore_wait(barrier, len(group) + len(across) + len(heads_z))

    def q_piece(x2, yp2, c2):
        return qq_hbm.at[0, pl.ds(pl.multiple_of(HALF * yp2, HALF), HALF),
                         pl.ds(pl.multiple_of(DH * (x2 * 2 + c2), DH), DH)]

    def kv_piece(x2, yp2, c2):
        return qkv_hbm.at[0, c2, pl.ds(pl.multiple_of(16 * (x2 * 2 + yp2), 16), 16), :]

    def block_rows(g):
        return kvall.at[:, pl.ds(pl.multiple_of(BLK * g, BLK), BLK), :]

    for dx, dp, dc, x2, yp2, c2, target in group:
        send(q_piece(x2, yp2, c2), q1buf.at[gid], q1_s, q1_r, target)
    local(q_piece(x, yp, c), q1buf.at[gid], q1_r)
    for dx, dp, dc, x2, yp2, c2, target in group:
        send(kv_piece(x2, yp2, c2), r1buf.at[gid], r1_s, r1_r, target)
    local(kv_piece(x, yp, c), r1buf.at[gid], r1_r)

    @pl.when(ctx == 0)
    def _():
        for target in across:
            send(ckv_hbm, akv.at[:, pl.ds(0, BLK), :], a1_s, a1_r, target)
        local(ckv_hbm, akv.at[:, pl.ds(0, BLK), :], a1_r)

    for dx, dp, dc, x2, yp2, c2, target in group:
        if dc == 0:
            send(ckv_hbm, block_rows(gid), kv_s, kv_r, target)
    local(ckv_hbm, block_rows(gid), kv_r)

    host = host_ref[0]
    length = len_ref[0]
    host_y = (host // 2) % NY
    host_pg = host_y // 2
    host_g = (host % 2) * 8 + (host // 16) * 2 + host_y % 2

    drain(q1buf, q1_r)
    q1sel[...] = q1buf[host_g]
    for target in across:
        send(q1sel, q2buf.at[pg], q2_s, q2_r, target)
    local(q1sel, q2buf.at[pg], q2_r)

    drain(r1buf, r1_r)
    r1sel[...] = r1buf[host_g]
    r2dst = kvall.at[c, pl.ds(pl.multiple_of(GROUP * BLK + 16 * (x * 2 + yp), 16), 16), :]
    for dx, dp, dc, x2, yp2, c2, target in group:
        send(r1sel, r2dst, r2_s, r2_r, target)
    local(r1sel, r2dst, r2_r)

    half_blocks = kvall.at[:, pl.ds(pl.multiple_of(8 * BLK * c, BLK), 8 * BLK), :]
    drain(half_blocks, kv_r)
    send(half_blocks, half_blocks, km_s, km_r, mate)

    is_source = (x == 0) & (yp == 0) & (c == 0)
    anchor_rows = akv.at[:, pl.ds(0, BLK), :]

    @pl.when(is_source)
    def _():
        drain(anchor_rows, a1_r)
        for dx, dp, dc, x2, yp2, c2, target in group:
            if dc == 0:
                send(anchor_rows, anchor_rows, a2_s, a2_r, target)

    drain(q2buf, q2_r)
    drain(kvall.at[:, pl.ds(GROUP * BLK, BLK), :], r2_r)
    drain(half_blocks, km_r)

    qsel = q2buf[host_pg]
    raw = dot_t(qsel, kvall[0])
    keys_n = (GROUP + 1) * BLK
    col = lax.broadcasted_iota(jnp.int32, (HALF, BLK), 1)
    row = lax.broadcasted_iota(jnp.int32, (HALF, BLK), 0) + HALF * yp
    limit = jnp.where(host_pg == pg, length, 0)
    own = jnp.where((col <= row) & (col < limit), raw[:, GROUP * BLK:], MASKED)
    raw = jnp.concatenate([raw[:, : GROUP * BLK], own], axis=1)
    top = jnp.max(raw, axis=1, keepdims=True)
    wts = jnp.exp2((raw - top) * COEF)
    tot = jnp.sum(wts, axis=1, keepdims=True)
    num = jnp.dot(wts.astype(jnp.bfloat16), kvall[1], preferred_element_type=jnp.float32)
    pbuf[pg] = (num / tot).astype(jnp.bfloat16)
    lse = top * COEF + jnp.log(tot) * LOG2E
    row64 = lax.broadcasted_iota(jnp.int32, (HALF, BLK), 0)
    diag = col == row64
    lse_row = jnp.sum(jnp.where(diag, lse, 0.0), axis=0, keepdims=True)
    lbuf[pg] = jnp.broadcast_to(lse_row, (8, BLK))
    for target in across:
        send(lbuf.at[pg], lbuf.at[pg], l_s, l_r, target)
        send(pbuf.at[pg], pbuf.at[pg], p_s, p_r, target)

    @pl.when(c == 0)
    def _():
        @pl.when(jnp.logical_not(is_source))
        def _():
            drain(anchor_rows, a2_r)

        send(anchor_rows, anchor_rows, am_s, am_r, mate)

    load_q.wait()
    load_own.wait()

    drain(lbuf.at[pl.ds(0, 3)], l_r)
    drain(pbuf.at[pl.ds(0, 3)], p_r)
    rows4 = [lbuf[i][0:1, :] for i in range(NPG)]
    best = jnp.maximum(jnp.maximum(rows4[0], rows4[1]), jnp.maximum(rows4[2], rows4[3]))
    fac = [jnp.exp2(r - best) for r in rows4]
    inv = 1.0 / (fac[0] + fac[1] + fac[2] + fac[3])
    attn = jnp.zeros((HALF, DH), jnp.float32)
    for i in range(NPG):
        fcol = jnp.sum(jnp.where(diag, fac[i] * inv, 0.0), axis=1, keepdims=True)
        attn = attn + fcol * pbuf[i].astype(jnp.float32)
    attn = jnp.where(row < length, attn, 0.0).astype(jnp.bfloat16)
    mine = abuf.at[pl.ds(pl.multiple_of(HALF * yp, HALF), HALF), pl.ds(pl.multiple_of(DH * head, DH), DH)]
    mine[...] = attn
    for dx, dp, dc, x2, yp2, c2, target in group:
        send(mine, mine, g_s, g_r, target)

    @pl.when(c == 1)
    def _():
        drain(anchor_rows, am_r)

    ccol = lax.broadcasted_iota(jnp.int32, (BLK, 2 * BLK), 1)
    crow = lax.broadcasted_iota(jnp.int32, (BLK, 2 * BLK), 0)
    first_visible = jnp.where(ctx > 0, 0, BLK)
    visible = (ccol >= first_visible) & (ccol - BLK <= crow)

    def context_heads(lo, hi):
        for h in range(lo, hi):
            sc = dot_t(cq[:, h * DH:(h + 1) * DH], akv[0])
            sc = jnp.where(visible, sc, MASKED)
            mx = jnp.max(sc, axis=1, keepdims=True)
            pw = jnp.exp2((sc - mx) * COEF)
            tl = jnp.sum(pw, axis=1, keepdims=True)
            nm = jnp.dot(pw.astype(jnp.bfloat16), akv[1], preferred_element_type=jnp.float32)
            cout[:, h * DH:(h + 1) * DH] = (nm / tl).astype(jnp.bfloat16)

    context_heads(0, 4)

    load_w.wait()
    drain(q1buf.at[pl.ds(0, GROUP - 1)], g_r)
    zsrc[...] = jnp.dot(abuf[...], w[...], preferred_element_type=jnp.float32).astype(jnp.bfloat16)
    for z2, target in heads_z:
        send(zsrc.at[pl.ds(pl.multiple_of(16 * z2, 16), 16), :], zbuf.at[z], z_s, z_r, target)
    zbuf[z] = zsrc[pl.ds(pl.multiple_of(16 * z, 16), 16), :]

    context_heads(4, 8)
    store_c = local(cout, cout_hbm, osem)

    drain(q1buf.at[pl.ds(0, GROUP - 1)], q1_s)
    drain(r1buf.at[pl.ds(0, GROUP - 1)], r1_s)
    drain(r1buf.at[pl.ds(0, GROUP - 1)], r2_s)
    drain(kvall.at[:, pl.ds(0, 7 * BLK), :], kv_s)
    drain(half_blocks, km_s)
    drain(q2buf.at[pl.ds(0, 3)], q2_s)
    drain(pbuf.at[pl.ds(0, 3)], p_s)
    drain(lbuf.at[pl.ds(0, 3)], l_s)
    drain(q1buf.at[pl.ds(0, GROUP - 1)], g_s)

    @pl.when(ctx == 0)
    def _():
        drain(kvall.at[:, pl.ds(0, 3 * BLK), :], a1_s)

    @pl.when(is_source)
    def _():
        drain(kvall.at[:, pl.ds(0, 7 * BLK), :], a2_s)

    @pl.when(c == 0)
    def _():
        drain(anchor_rows, am_s)

    drain(zbuf.at[pl.ds(0, 7)], z_r)
    total = zbuf[0].astype(jnp.float32)
    for i in range(1, NZ):
        total = total + zbuf[i].astype(jnp.float32)
    qout_ref[...] = total.astype(jnp.bfloat16)
    drain(zbuf.at[pl.ds(0, 7)], z_s)
    store_c.wait()


def per_device(ctx_q, ctx_kv, quest_q, quest_kv, quest_len, host_block, out_weight):
    bf = jnp.bfloat16
    any_spec = pl.BlockSpec(memory_space=pl.ANY)
    smem = pl.BlockSpec(memory_space=pltpu.SMEM)
    dma = pltpu.SemaphoreType.DMA
    return pl.pallas_call(
        kernel,
        out_shape=(
            jax.ShapeDtypeStruct((BLK, HEADS * DH), bf),
            jax.ShapeDtypeStruct((BLK // NZ, DH), bf),
        ),
        in_specs=[smem, smem] + [any_spec] * 5,
        out_specs=(any_spec, pl.BlockSpec(memory_space=pltpu.VMEM)),
        scratch_shapes=[
            pltpu.VMEM((BLK, HEADS * DH), bf),
            pltpu.VMEM((HEADS * DH, DH), bf),
            pltpu.VMEM((2, 2 * BLK, DH), bf),
            pltpu.VMEM((2, (GROUP + 1) * BLK, DH), bf),
            pltpu.VMEM((GROUP, HALF, DH), bf),
            pltpu.VMEM((HALF, DH), bf),
            pltpu.VMEM((NPG, HALF, DH), bf),
            pltpu.VMEM((GROUP, 16, DH), bf),
            pltpu.VMEM((16, DH), bf),
            pltpu.VMEM((NPG, HALF, DH), bf),
            pltpu.VMEM((NPG, 8, DH), jnp.float32),
            pltpu.VMEM((BLK, HEADS * DH), bf),
            pltpu.VMEM((BLK, DH), bf),
            pltpu.VMEM((NZ, 16, DH), bf),
            pltpu.VMEM((BLK, HEADS * DH), bf),
            dma((3,)),
        ] + [dma] * 27,
        compiler_params=pltpu.CompilerParams(
            collective_id=0, has_side_effects=True, vmem_limit_bytes=48 * 1024 * 1024
        ),
        name="star_attention",
    )(quest_len, host_block, ctx_q, ctx_kv, quest_q, quest_kv, out_weight)


def solution(mesh):
    return jax.shard_map(
        per_device,
        mesh=mesh,
        in_specs=(
            P("ctx", "kvh"),
            P(None, "ctx", "kvh"),
            P("ctx", None, "kvh"),
            P("ctx", None, None, "kvh"),
            P(),
            P(),
            P("kvh", "ctx"),
        ),
        out_specs=(P("ctx", "kvh"), P("kvh", "ctx")),
        check_vma=False,
    )
```

time: 591 us -> 53.4 us (0.09); the launches traced: 585 us -> 53 us
  waiting for transfers between devices: 280 us -> 0 us
  blocking collectives: 251 us -> 0 us
  Pallas kernels: 0 us -> 45.3 us
  matrix products: 29.1 us -> 0 us
  between operations: 15.3 us -> 1.94 us
    psum x2 -> x0, waiting for transfers between devices: 256 us -> none  [the longest x1 195 us: from_root(): return lax.psum(block, axis)]
    psum x1 -> x0, blocking collectives: 126 us -> none  [per_device(): lax.psum((totals * factor, numers * jnp.repeat(factor, DH, axis=1)), 'ctx')]
    pmax x1 -> x0, blocking collectives: 125 us -> none  [per_device(): overall = lax.pmax(maxima, 'ctx')]
    pallas_call x0 -> x1, Pallas kernels: none -> 45.3 us  [per_device(): pl.pallas_call(kernel, out_shape=(jax.ShapeDtypeStruct((BLK, HEADS * DH),...]
    dot_general x49 -> x0, matrix products: 29.1 us -> none  [the longest x24 23.1 us: head_scores(): jnp.dot(queries, key_rows.T, preferred_element_type=jnp.float32)]
    reduce_scatter x1 -> x0, waiting for transfers between devices: 23.5 us -> none  [per_device(): lax.psum_scatter(jnp.dot(attn, out_weight, preferred_element_type=jnp.flo...]
  transfers between devices with their start and end apart: 3 -> 0, of which waited for: 3 -> 0; matrix products, arithmetic and copies ran while one was open for 2% -> 0% of each run, Pallas kernels for 0% -> 0%
where the time goes in v1:
time: 53.4 us; the launch traced here: 53 us
  Pallas kernels  45.3 us (85%)
  local copies, waits for them, and re-layouts  5.82 us (11%)
  between operations  1.94 us (4%)
    pallas_call x1, Pallas kernels, per_device(): pl.pallas_call(kernel, out_shape=(jax.ShapeDtypeStruct((BLK, HEADS * DH),...  45.3 us
    unnamed x12, local copies, waits for them, and re-layouts  5.82 us

profile of v1, /device:TPU:1, one launch (start us, length us, event | category | flops | bytes accessed | tf_op | source)
XLA Modules:
  0.0 53.0 jit_solution(14259321926943763222)
XLA Ops:
  1.9 0.0 copy-start
  1.9 0.9 %copy-done = bf16[128,1024]{1,0:T(8,128)(2,1)S(1)} copy-done((bf16[128,1024]{1,0:T(8,128)(2,1)S(1)}, bf16[128,1024]{1,0:T(8,128)(2,1)}, u32[]{:S(2)}) %copy-start) | copy-done | bytes 262168
  2.9 0.0 copy-start.1
  2.9 0.9 %copy-done.1 = bf16[1,128,1024]{2,1,0:T(8,128)(2,1)S(1)} copy-done((bf16[1,128,1024]{2,1,0:T(8,128)(2,1)S(1)}, bf16[1,128,1024]{2,1,0:T(8,128)(2,1)}, u32[]{:S(2)}) %copy-start.1) | copy-done | bytes 262168
  3.8 0.0 copy-start.2
  3.8 0.9 %copy-done.2 = bf16[1024,128]{1,0:T(8,128)(2,1)S(1)} copy-done((bf16[1024,128]{1,0:T(8,128)(2,1)S(1)}, bf16[1024,128]{1,0:T(8,128)(2,1)}, u32[]{:S(2)}) %copy-start.2) | copy-done | bytes 262168
  4.8 0.0 copy-start.3
  4.8 0.8 %copy-done.3 = bf16[2,128,128]{2,1,0:T(8,128)(2,1)S(1)} copy-done((bf16[2,128,128]{2,1,0:T(8,128)(2,1)S(1)}, bf16[2,128,128]{2,1,0:T(8,128)(2,1)}, u32[]{:S(2)}) %copy-start.3) | copy-done | bytes 65560
  5.6 0.0 copy-start.4
  5.6 0.8 %copy-done.4 = bf16[1,2,128,128]{3,2,1,0:T(8,128)(2,1)S(1)} copy-done((bf16[1,2,128,128]{3,2,1,0:T(8,128)(2,1)S(1)}, bf16[1,2,128,128]{3,2,1,0:T(8,128)(2,1)}, u32[]{:S(2)}) %copy-start.4) | copy-done | bytes 65560
  6.5 45.3 %star_attention.1 = (bf16[128,1024]{1,0:T(8,128)(2,1)S(1)}, bf16[16,128]{1,0:T(8,128)(2,1)S(1)}) custom-call(s32[1]{0:T(128)S(6)} %copy.11.len_ref, s32[1]{0:T(128)S(6)} %copy.12.host_ref, bf16[128,1024]{1,0:T(8,128)(2,1)S(1)} %copy-done, bf16[2,128,128]{2,1,0:T(8,128)(2,1)S(1)} %copy-done.3, bf16[1,128,1024]{2,1,0:T(8,128)(2,1)S(1)} %copy-done.1, ...), custom_call_target="tpu_custom_call" | custom-call | tf_op jit(solution)/shard_map/star_attention/pallas_call | solution.py:269
  51.7 0.7 %copy.13 = bf16[128,1024]{1,0:T(8,128)(2,1)} copy(bf16[128,1024]{1,0:T(8,128)(2,1)S(1)} %get-tuple-element.4) | data formatting | bytes 524288
  52.5 0.6 %copy.14 = bf16[16,128]{1,0:T(8,128)(2,1)} copy(bf16[16,128]{1,0:T(8,128)(2,1)S(1)} %get-tuple-element.5) | data formatting | bytes 8192
Async XLA Ops:
  1.9 1.0 %copy-start = (bf16[128,1024]{1,0:T(8,128)(2,1)S(1)}, bf16[128,1024]{1,0:T(8,128)(2,1)}, u32[]{:S(2)}) copy-start(bf16[128,1024]{1,0:T(8,128)(2,1)} %cq_hbm.1) | copy-start | bytes 786436
  2.9 0.9 %copy-start.1 = (bf16[1,128,1024]{2,1,0:T(8,128)(2,1)S(1)}, bf16[1,128,1024]{2,1,0:T(8,128)(2,1)}, u32[]{:S(2)}) copy-start(bf16[1,128,1024]{2,1,0:T(8,128)(2,1)} %qq_hbm.1) | copy-start | bytes 786436
  3.8 0.9 %copy-start.2 = (bf16[1024,128]{1,0:T(8,128)(2,1)S(1)}, bf16[1024,128]{1,0:T(8,128)(2,1)}, u32[]{:S(2)}) copy-start(bf16[1024,128]{1,0:T(8,128)(2,1)} %w_hbm.1) | copy-start | bytes 786436
  4.8 0.8 %copy-start.3 = (bf16[2,128,128]{2,1,0:T(8,128)(2,1)S(1)}, bf16[2,128,128]{2,1,0:T(8,128)(2,1)}, u32[]{:S(2)}) copy-start(bf16[2,128,128]{2,1,0:T(8,128)(2,1)} %ckv_hbm.1) | copy-start | bytes 196612
  5.6 0.8 %copy-start.4 = (bf16[1,2,128,128]{3,2,1,0:T(8,128)(2,1)S(1)}, bf16[1,2,128,128]{3,2,1,0:T(8,128)(2,1)}, u32[]{:S(2)}) copy-start(bf16[1,2,128,128]{3,2,1,0:T(8,128)(2,1)} %qkv_hbm.1) | copy-start | bytes 196612

commit v2 on v1

v2 whole, which is shorter than its diff:
```python
import functools
import math

import jax
import jax.numpy as jnp
from jax import lax
from jax.experimental import pallas as pl
from jax.experimental.pallas import tpu as pltpu
from jax.sharding import PartitionSpec as P


DH = 128
BLK = 128
HEADS = 8
HALF = 64
NX, NY, NZ = 4, 8, 8
ROW = 8
NPG = 4
MASKED = -1e30
SCALE = DH ** (-0.5)
LOG2E = math.log2(math.e)
COEF = SCALE * LOG2E
MESH = pl.DeviceIdType.MESH


def dot_t(a, b):
    return lax.dot_general(a, b, (((1,), (1,)), ((), ())), preferred_element_type=jnp.float32)


def when(cond):
    if cond is None:
        return lambda f: f()
    return pl.when(cond)


def kernel(
    hx, hpg,
    len_ref, host_ref, cq_hbm, ckv_hbm, qq_hbm, qkv_hbm, w_hbm,
    cout_hbm, qout_ref,
    cq, w, akv, kvall, q1buf, q1sel, q2buf, r1buf, r1sel, po, lsend, pbuf, lbuf, abuf, zsrc, zbuf, cout,
    lsem, zs, osem, q1_s, q1_r, q2_s, q2_r, r1_s, r1_r, r2_s, r2_r, kv_s, kv_r, km_s, km_r,
    a1_s, a1_r, a2_s, a2_r, am_s, am_r, p_s, p_r, l_s, l_r, g_s, g_r, z_s, z_r,
):
    ctx = lax.axis_index("ctx")
    z = lax.axis_index("kvh")
    x = ctx // 16
    y = (ctx // 2) % NY
    c = ctx % 2
    yp = y % 2
    pg = y // 2
    head = x * 2 + c

    def at(x2, y2, c2, z2):
        return ((x2 * NY + y2) * 2 + c2, z2)

    group = []
    for dx in (1, 3, 2, 0):
        for dp in range(2):
            for dc in range(2):
                if dx or dp or dc:
                    x2 = (x + dx) % NX
                    yp2 = (yp + dp) % 2
                    c2 = (c + dc) % 2
                    group.append((dp, dc, x2, yp2, c2, at(x2, pg * 2 + yp2, c2, z)))
    row_members = [m[1:] for m in group if m[0] == 0]
    same_core = [m[-1] for m in row_members if m[0] == 0]
    column = [((yp + k) % 2, at(x, (y + k) % NY, c, z)) for k in (4, 3, 5, 2, 6, 1, 7)]
    heads_z = [((z + k) % NZ, at(x, y, c, (z + k) % NZ)) for k in (1, 7, 2, 6, 3, 5, 4)]
    z_near = [t for _, t in heads_z[:2]]
    mate = at(x, y, 1 - c, z)

    in_pg = None if hpg is None else pg == hpg
    sender = in_pg
    if hx is not None:
        sender = x == hx if sender is None else sender & (x == hx)
    q1_slots = 16 if hx is None else 4
    r1_slots = 8 if hx is None else 2
    q1_slot = c * 8 + x * 2 + yp if hx is None else c * 2 + yp
    r1_slot = c * 4 + x if hx is None else c

    def local(src, dst, sem):
        cp = pltpu.make_async_copy(src, dst, sem)
        cp.start()
        return cp

    def send(src, dst, ssem, rsem, target):
        pltpu.make_async_remote_copy(
            src_ref=src, dst_ref=dst, send_sem=ssem, recv_sem=rsem, device_id=target, device_id_type=MESH
        ).start()

    def drain(ref, sem):
        pltpu.make_async_copy(ref, ref, sem).wait()

    def halves(n):
        return kvall.at[0, pl.ds(0, n * HALF), :]

    def near_signal(i):
        for t in z_near:
            pl.semaphore_signal(zs.at[i], inc=1, device_id=t, device_id_type=MESH)

    load_q = local(cq_hbm, cq, lsem.at[0])
    load_own = local(ckv_hbm, akv.at[:, pl.ds(BLK, BLK), :], lsem.at[1])
    load_w = local(w_hbm, w, lsem.at[2])

    barrier = pltpu.get_barrier_semaphore()
    greet = [m[-1] for m in group] + [t for _, t in column] + z_near
    for t in greet:
        pl.semaphore_signal(barrier, inc=1, device_id=t, device_id_type=MESH)
    pl.semaphore_wait(barrier, len(greet))
    near_signal(0)

    def q_piece(x2, yp2, c2):
        return qq_hbm.at[0, pl.ds(pl.multiple_of(HALF * yp2, HALF), HALF),
                         pl.ds(pl.multiple_of(DH * (x2 * 2 + c2), DH), DH)]

    def kv_piece(x2, c2):
        first = pl.multiple_of(32 * (c2 * 2 + x2 % 2), 32)
        return qkv_hbm.at[0, x2 // 2, pl.ds(first, 32), :]

    block_rows = kvall.at[:, pl.ds(pl.multiple_of(BLK * (c * 4 + x), BLK), BLK), :]

    @when(sender)
    def _():
        for dc, x2, yp2, c2, target in row_members:
            send(kv_piece(x2, c2), r1buf.at[r1_slot], r1_s, r1_r, target)
        local(kv_piece(x, c), r1buf.at[r1_slot], r1_r)
        for dp, dc, x2, yp2, c2, target in group:
            send(q_piece(x2, yp2, c2), q1buf.at[q1_slot], q1_s, q1_r, target)
        local(q_piece(x, yp, c), q1buf.at[q1_slot], q1_r)

    for target in same_core:
        send(ckv_hbm, block_rows, kv_s, kv_r, target)
    local(ckv_hbm, block_rows, kv_r)

    anchor_rows = akv.at[:, pl.ds(0, BLK), :]

    @pl.when(ctx == 0)
    def _():
        for _, target in column:
            send(ckv_hbm, anchor_rows, a1_s, a1_r, target)
        local(ckv_hbm, anchor_rows, a1_r)

    host = host_ref[0]
    length = len_ref[0]
    host_x = host // 16
    host_y = (host // 2) % NY
    host_c = host % 2
    host_yp = host_y % 2
    host_q1 = host_c * 8 + host_x * 2 + host_yp if hx is None else host_c * 2 + host_yp
    host_r1 = host_c * 4 + host_x if hx is None else host_c

    own_rows = kvall.at[:, pl.ds(ROW * BLK, BLK), :]
    r2dst = kvall.at[x // 2, pl.ds(pl.multiple_of(ROW * BLK + 32 * (c * 2 + x % 2), 32), 32), :]
    half_blocks = kvall.at[:, pl.ds(pl.multiple_of(4 * BLK * c, BLK), 4 * BLK), :]
    q2dst = q2buf.at[pg if hpg is None else 0, pl.ds(pl.multiple_of(HALF * yp, HALF), HALF), :]

    @when(in_pg)
    def _():
        drain(r1buf, r1_r)
        r1sel[...] = r1buf[host_r1]
        for dc, x2, yp2, c2, target in row_members:
            send(r1sel, r2dst, r2_s, r2_r, target)
        local(r1sel, r2dst, r2_r)
        drain(q1buf, q1_r)
        q1sel[...] = q1buf[host_q1]
        for _, target in column:
            send(q1sel, q2dst, q2_s, q2_r, target)
        local(q1sel, q2dst, q2_r)

    if hpg is not None:
        @pl.when(pg != hpg)
        def _():
            own_rows[...] = jnp.zeros((2, BLK, DH), jnp.bfloat16)

    drain(half_blocks, kv_r)
    send(half_blocks, half_blocks, km_s, km_r, mate)

    is_source = (x == 0) & (c == 0)

    @pl.when(is_source)
    def _():
        drain(anchor_rows, a1_r)
        for target in same_core:
            send(anchor_rows, anchor_rows, a2_s, a2_r, target)

    pl.semaphore_wait(zs.at[0], 2)
    near_signal(1)

    drain(half_blocks, km_r)

    @when(in_pg)
    def _():
        drain(own_rows, r2_r)

    drain(q2buf, q2_r)

    qsel = q2buf[host_y // 2] if hpg is None else q2buf[0]
    raw = dot_t(qsel, kvall[0])
    col = lax.broadcasted_iota(jnp.int32, (BLK, BLK), 1)
    row = lax.broadcasted_iota(jnp.int32, (BLK, BLK), 0)
    limit = jnp.where(host_y == y, length, 0)
    own = jnp.where((col <= row) & (col < limit), raw[:, ROW * BLK:], MASKED)
    raw = jnp.concatenate([raw[:, : ROW * BLK], own], axis=1)
    top = jnp.max(raw, axis=1, keepdims=True)
    wts = jnp.exp2((raw - top) * COEF)
    tot = jnp.sum(wts, axis=1, keepdims=True)
    num = jnp.dot(wts.astype(jnp.bfloat16), kvall[1], preferred_element_type=jnp.float32)
    po[...] = (num / tot).astype(jnp.bfloat16)
    lse = top * COEF + jnp.log(tot) * LOG2E
    lse_row = jnp.sum(jnp.where(col == row, lse, 0.0), axis=0, keepdims=True)
    lse_tile = jnp.broadcast_to(lse_row, (8, BLK))
    lsend[...] = lse_tile
    lbuf[y] = lse_tile
    for h2, target in column:
        send(lsend, lbuf.at[y], l_s, l_r, target)
        send(po.at[pl.ds(pl.multiple_of(HALF * h2, HALF), HALF), :], pbuf.at[y], p_s, p_r, target)
    pbuf[y] = po[pl.ds(pl.multiple_of(HALF * yp, HALF), HALF), :]

    @pl.when(c == 0)
    def _():
        @pl.when(jnp.logical_not(is_source))
        def _():
            drain(anchor_rows, a2_r)

        send(anchor_rows, anchor_rows, am_s, am_r, mate)

    load_q.wait()
    load_own.wait()
    pl.semaphore_wait(zs.at[1], 2)
    near_signal(2)

    drain(lbuf.at[pl.ds(0, NY - 1)], l_r)
    drain(pbuf.at[pl.ds(0, NY - 1)], p_r)
    lses = [lbuf[i][0:1, :] for i in range(NY)]
    best = functools.reduce(jnp.maximum, lses)
    fac = [jnp.exp2(v - best) for v in lses]
    inv = 1.0 / functools.reduce(jnp.add, fac)
    hcol = lax.broadcasted_iota(jnp.int32, (HALF, BLK), 1)
    hrow = lax.broadcasted_iota(jnp.int32, (HALF, BLK), 0) + HALF * yp
    diag = hcol == hrow
    attn = jnp.zeros((HALF, DH), jnp.float32)
    for i in range(NY):
        fcol = jnp.sum(jnp.where(diag, fac[i] * inv, 0.0), axis=1, keepdims=True)
        attn = attn + fcol * pbuf[i].astype(jnp.float32)
    attn = jnp.where(hrow < length, attn, 0.0).astype(jnp.bfloat16)
    mine = abuf.at[pl.ds(pl.multiple_of(HALF * yp, HALF), HALF), pl.ds(pl.multiple_of(DH * head, DH), DH)]
    mine[...] = attn
    for dp, dc, x2, yp2, c2, target in group:
        send(mine, mine, g_s, g_r, target)

    @pl.when(c == 1)
    def _():
        drain(anchor_rows, am_r)

    ccol = lax.broadcasted_iota(jnp.int32, (BLK, 2 * BLK), 1)
    crow = lax.broadcasted_iota(jnp.int32, (BLK, 2 * BLK), 0)
    first_visible = jnp.where(ctx > 0, 0, BLK)
    visible = (ccol >= first_visible) & (ccol - BLK <= crow)

    def context_heads(lo, hi):
        for h in range(lo, hi):
            sc = dot_t(cq[:, h * DH:(h + 1) * DH], akv[0])
            sc = jnp.where(visible, sc, MASKED)
            mx = jnp.max(sc, axis=1, keepdims=True)
            pw = jnp.exp2((sc - mx) * COEF)
            tl = jnp.sum(pw, axis=1, keepdims=True)
            nm = jnp.dot(pw.astype(jnp.bfloat16), akv[1], preferred_element_type=jnp.float32)
            cout[:, h * DH:(h + 1) * DH] = (nm / tl).astype(jnp.bfloat16)

    context_heads(0, 4)

    load_w.wait()
    pl.semaphore_wait(zs.at[2], 2)
    drain(halves(15), g_r)
    zsrc[...] = jnp.dot(abuf[...], w[...], preferred_element_type=jnp.float32).astype(jnp.bfloat16)
    for z2, target in heads_z:
        send(zsrc.at[pl.ds(pl.multiple_of(16 * z2, 16), 16), :], zbuf.at[z], z_s, z_r, target)
    zbuf[z] = zsrc[pl.ds(pl.multiple_of(16 * z, 16), 16), :]

    context_heads(4, 8)
    store_c = local(cout, cout_hbm, osem)

    @when(sender)
    def _():
        drain(halves(15), q1_s)
        drain(kvall.at[0, pl.ds(0, 7 * 32), :], r1_s)

    @when(in_pg)
    def _():
        drain(kvall.at[0, pl.ds(0, 7 * 32), :], r2_s)
        drain(halves(7), q2_s)

    drain(kvall.at[:, pl.ds(0, 3 * BLK), :], kv_s)
    drain(half_blocks, km_s)
    drain(pbuf.at[pl.ds(0, NY - 1)], p_s)
    drain(lbuf.at[pl.ds(0, NY - 1)], l_s)
    drain(halves(15), g_s)

    @pl.when(ctx == 0)
    def _():
        drain(kvall.at[:, pl.ds(0, 7 * BLK), :], a1_s)

    @pl.when(is_source)
    def _():
        drain(kvall.at[:, pl.ds(0, 3 * BLK), :], a2_s)

    @pl.when(c == 0)
    def _():
        drain(anchor_rows, am_s)

    drain(zbuf.at[pl.ds(0, NZ - 1)], z_r)
    total = zbuf[0].astype(jnp.float32)
    for i in range(1, NZ):
        total = total + zbuf[i].astype(jnp.float32)
    qout_ref[...] = total.astype(jnp.bfloat16)
    drain(zbuf.at[pl.ds(0, NZ - 1)], z_s)
    store_c.wait()


def call(collective_id, hx, hpg, ctx_q, ctx_kv, quest_q, quest_kv, quest_len, host_block, out_weight):
    bf = jnp.bfloat16
    any_spec = pl.BlockSpec(memory_space=pl.ANY)
    smem = pl.BlockSpec(memory_space=pltpu.SMEM)
    dma = pltpu.SemaphoreType.DMA
    large = [pltpu.with_memory_space_constraint(v, pltpu.HBM) for v in (ctx_q, ctx_kv, quest_q, quest_kv, out_weight)]
    return pl.pallas_call(
        functools.partial(kernel, hx, hpg),
        out_shape=(
            jax.ShapeDtypeStruct((BLK, HEADS * DH), bf),
            jax.ShapeDtypeStruct((BLK // NZ, DH), bf),
        ),
        in_specs=[smem, smem] + [any_spec] * 5,
        out_specs=(any_spec, pl.BlockSpec(memory_space=pltpu.VMEM)),
        scratch_shapes=[
            pltpu.VMEM((BLK, HEADS * DH), bf),
            pltpu.VMEM((HEADS * DH, DH), bf),
            pltpu.VMEM((2, 2 * BLK, DH), bf),
            pltpu.VMEM((2, (ROW + 1) * BLK, DH), bf),
            pltpu.VMEM((16 if hx is None else 4, HALF, DH), bf),
            pltpu.VMEM((HALF, DH), bf),
            pltpu.VMEM((NPG if hpg is None else 1, BLK, DH), bf),
            pltpu.VMEM((8 if hx is None else 2, 32, DH), bf),
            pltpu.VMEM((32, DH), bf),
            pltpu.VMEM((BLK, DH), bf),
            pltpu.VMEM((8, BLK), jnp.float32),
            pltpu.VMEM((NY, HALF, DH), bf),
            pltpu.VMEM((NY, 8, BLK), jnp.float32),
            pltpu.VMEM((BLK, HEADS * DH), bf),
            pltpu.VMEM((BLK, DH), bf),
            pltpu.VMEM((NZ, 16, DH), bf),
            pltpu.VMEM((BLK, HEADS * DH), bf),
            dma((3,)),
            pltpu.SemaphoreType.REGULAR((3,)),
        ] + [dma] * 27,
        compiler_params=pltpu.CompilerParams(
            collective_id=collective_id, has_side_effects=True, vmem_limit_bytes=48 * 1024 * 1024
        ),
        name="star_attention",
    )(quest_len, host_block, *large)


def per_device(*args):
    return call(0, None, None, *args)


def solution(mesh):
    return jax.shard_map(
        per_device,
        mesh=mesh,
        in_specs=(
            P("ctx", "kvh"),
            P(None, "ctx", "kvh"),
            P("ctx", None, "kvh"),
            P("ctx", None, None, "kvh"),
            P(),
            P(),
            P("kvh", "ctx"),
        ),
        out_specs=(P("ctx", "kvh"), P("kvh", "ctx")),
        check_vma=False,
    )
```

time: 53.4 us -> 45.6 us (0.85)
  local copies, waits for them, and re-layouts: 5.82 us -> 1.3 us
  Pallas kernels: 45.3 us -> 42.3 us
    unnamed x12 -> x2, local copies, waits for them, and re-layouts: 5.82 us -> 1.3 us
    pallas_call x1, Pallas kernels: 45.3 us -> 42.3 us  [call(): pl.pallas_call(functools.partial(kernel, hx, hpg), out_shape=(jax.ShapeDt...]
where the time goes in v2:
time: 45.6 us; the launch traced here: 45.5 us
  Pallas kernels  42.3 us (93%)
  between operations  1.93 us (4%)
  local copies, waits for them, and re-layouts  1.3 us (3%)
    pallas_call x1, Pallas kernels, call(): pl.pallas_call(functools.partial(kernel, hx, hpg), out_shape=(jax.ShapeDt...  42.3 us
    unnamed x2, local copies, waits for them, and re-layouts  1.3 us

profile of v2, /device:TPU:1, one launch (start us, length us, event | category | flops | bytes accessed | tf_op | source)
XLA Modules:
  0.0 45.5 jit_solution(16796947318054949347)
XLA Ops:
  1.9 42.3 %star_attention.1 = (bf16[128,1024]{1,0:T(8,128)(2,1)S(1)}, bf16[16,128]{1,0:T(8,128)(2,1)S(1)}) custom-call(s32[1]{0:T(128)S(6)} %copy.11.len_ref, s32[1]{0:T(128)S(6)} %copy.12.host_ref, bf16[128,1024]{1,0:T(8,128)(2,1)} %cq_hbm.1, bf16[2,128,128]{2,1,0:T(8,128)(2,1)} %ckv_hbm.1, bf16[1,128,1024]{2,1,0:T(8,128)(2,1)} %qq_hbm.1, ...), custom_call_target="tpu_custom_call" | custom-call | tf_op jit(solution)/shard_map/star_attention/pallas_call | solution.py:326
  44.2 0.7 %copy.13 = bf16[128,1024]{1,0:T(8,128)(2,1)} copy(bf16[128,1024]{1,0:T(8,128)(2,1)S(1)} %get-tuple-element.4) | data formatting | bytes 524288
  44.9 0.6 %copy.14 = bf16[16,128]{1,0:T(8,128)(2,1)} copy(bf16[16,128]{1,0:T(8,128)(2,1)S(1)} %get-tuple-element.5) | data formatting | bytes 8192

commit v3 on v2

--- a/solution.py
+++ b/solution.py
@@ -38,7 +38,7 @@
     len_ref, host_ref, cq_hbm, ckv_hbm, qq_hbm, qkv_hbm, w_hbm,
     cout_hbm, qout_ref,
     cq, w, akv, kvall, q1buf, q1sel, q2buf, r1buf, r1sel, po, lsend, pbuf, lbuf, abuf, zsrc, zbuf, cout,
-    lsem, zs, osem, q1_s, q1_r, q2_s, q2_r, r1_s, r1_r, r2_s, r2_r, kv_s, kv_r, km_s, km_r,
+    lsem, zs, ys, osem, q1_s, q1_r, q2_s, q2_r, r1_s, r1_r, r2_s, r2_r, kv_s, kv_r, km_s, km_r,
     a1_s, a1_r, a2_s, a2_r, am_s, am_r, p_s, p_r, l_s, l_r, g_s, g_r, z_s, z_r,
 ):
     ctx = lax.axis_index("ctx")
@@ -54,8 +54,8 @@
         return ((x2 * NY + y2) * 2 + c2, z2)
 
     group = []
-    for dx in (1, 3, 2, 0):
-        for dp in range(2):
+    for dx in (2, 1, 3, 0):
+        for dp in (1, 0):
             for dc in range(2):
                 if dx or dp or dc:
                     x2 = (x + dx) % NX
@@ -65,8 +65,10 @@
     row_members = [m[1:] for m in group if m[0] == 0]
     same_core = [m[-1] for m in row_members if m[0] == 0]
     column = [((yp + k) % 2, at(x, (y + k) % NY, c, z)) for k in (4, 3, 5, 2, 6, 1, 7)]
-    heads_z = [((z + k) % NZ, at(x, y, c, (z + k) % NZ)) for k in (1, 7, 2, 6, 3, 5, 4)]
-    z_near = [t for _, t in heads_z[:2]]
+    heads_z = [((z + k) % NZ, at(x, y, c, (z + k) % NZ)) for k in (4, 3, 5, 2, 6, 1, 7)]
+    z_near = [t for _, t in heads_z[-2:]]
+    y_near = [at(x, (y + 1) % NY, c, z), at(x, (y + NY - 1) % NY, c, z)]
+    y_out = at(x, (y + 2 * yp + NY - 1) % NY, c, z)
     mate = at(x, y, 1 - c, z)
 
     in_pg = None if hpg is None else pg == hpg
@@ -94,21 +96,18 @@
     def halves(n):
         return kvall.at[0, pl.ds(0, n * HALF), :]
 
-    def near_signal(i):
-        for t in z_near:
-            pl.semaphore_signal(zs.at[i], inc=1, device_id=t, device_id_type=MESH)
-
+    def near_signal(sem, i, near):
+        for t in near:
+            pl.semaphore_signal(sem.at[i], inc=1, device_id=t, device_id_type=MESH)
+
+    barrier = pltpu.get_barrier_semaphore()
+    greet = [m[-1] for m in group] + [y_out] + z_near
+    for t in greet:
+        pl.semaphore_signal(barrier, inc=1, device_id=t, device_id_type=MESH)
     load_q = local(cq_hbm, cq, lsem.at[0])
     load_own = local(ckv_hbm, akv.at[:, pl.ds(BLK, BLK), :], lsem.at[1])
     load_w = local(w_hbm, w, lsem.at[2])
-
-    barrier = pltpu.get_barrier_semaphore()
-    greet = [m[-1] for m in group] + [t for _, t in column] + z_near
-    for t in greet:
-        pl.semaphore_signal(barrier, inc=1, device_id=t, device_id_type=MESH)
     pl.semaphore_wait(barrier, len(greet))
-    near_signal(0)
-
     def q_piece(x2, yp2, c2):
         return qq_hbm.at[0, pl.ds(pl.multiple_of(HALF * yp2, HALF), HALF),
                          pl.ds(pl.multiple_of(DH * (x2 * 2 + c2), DH), DH)]
@@ -121,12 +120,19 @@
 
     @when(sender)
     def _():
+        for dp, dc, x2, yp2, c2, target in group:
+            send(q_piece(x2, yp2, c2), q1buf.at[q1_slot], q1_s, q1_r, target)
+        local(q_piece(x, yp, c), q1buf.at[q1_slot], q1_r)
+
+    near_signal(ys, 0, y_near)
+
+    @when(sender)
+    def _():
         for dc, x2, yp2, c2, target in row_members:
             send(kv_piece(x2, c2), r1buf.at[r1_slot], r1_s, r1_r, target)
         local(kv_piece(x, c), r1buf.at[r1_slot], r1_r)
-        for dp, dc, x2, yp2, c2, target in group:
-            send(q_piece(x2, yp2, c2), q1buf.at[q1_slot], q1_s, q1_r, target)
-        local(q_piece(x, yp, c), q1buf.at[q1_slot], q1_r)
+
+    near_signal(zs, 0, z_near)
 
     for target in same_core:
         send(ckv_hbm, block_rows, kv_s, kv_r, target)
@@ -134,11 +140,10 @@
 
     anchor_rows = akv.at[:, pl.ds(0, BLK), :]
 
-    @pl.when(ctx == 0)
-    def _():
-        for _, target in column:
-            send(ckv_hbm, anchor_rows, a1_s, a1_r, target)
-        local(ckv_hbm, anchor_rows, a1_r)
+    own_rows = kvall.at[:, pl.ds(ROW * BLK, BLK), :]
+    r2dst = kvall.at[x // 2, pl.ds(pl.multiple_of(ROW * BLK + 32 * (c * 2 + x % 2), 32), 32), :]
+    half_blocks = kvall.at[:, pl.ds(pl.multiple_of(4 * BLK * c, BLK), 4 * BLK), :]
+    q2dst = q2buf.at[pg if hpg is None else 0, pl.ds(pl.multiple_of(HALF * yp, HALF), HALF), :]
 
     host = host_ref[0]
     length = len_ref[0]
@@ -148,11 +153,24 @@
     host_yp = host_y % 2
     host_q1 = host_c * 8 + host_x * 2 + host_yp if hx is None else host_c * 2 + host_yp
     host_r1 = host_c * 4 + host_x if hx is None else host_c
-
-    own_rows = kvall.at[:, pl.ds(ROW * BLK, BLK), :]
-    r2dst = kvall.at[x // 2, pl.ds(pl.multiple_of(ROW * BLK + 32 * (c * 2 + x % 2), 32), 32), :]
-    half_blocks = kvall.at[:, pl.ds(pl.multiple_of(4 * BLK * c, BLK), 4 * BLK), :]
-    q2dst = q2buf.at[pg if hpg is None else 0, pl.ds(pl.multiple_of(HALF * yp, HALF), HALF), :]
+    pl.semaphore_wait(ys.at[0], 2)
+    near_signal(ys, 1, y_near)
+
+    pl.semaphore_wait(ys.at[1], 2)
+    near_signal(ys, 2, y_near)
+
+    @when(in_pg)
+    def _():
+        drain(q1buf, q1_r)
+        q1sel[...] = q1buf[host_q1]
+
+    pl.semaphore_wait(ys.at[2], 2)
+
+    @when(in_pg)
+    def _():
+        for _, target in column:
+            send(q1sel, q2dst, q2_s, q2_r, target)
+        local(q1sel, q2dst, q2_r)
 
     @when(in_pg)
     def _():
@@ -161,11 +179,12 @@
         for dc, x2, yp2, c2, target in row_members:
             send(r1sel, r2dst, r2_s, r2_r, target)
         local(r1sel, r2dst, r2_r)
-        drain(q1buf, q1_r)
-        q1sel[...] = q1buf[host_q1]
+
+    @pl.when(ctx == 0)
+    def _():
         for _, target in column:
-            send(q1sel, q2dst, q2_s, q2_r, target)
-        local(q1sel, q2dst, q2_r)
+            send(ckv_hbm, anchor_rows, a1_s, a1_r, target)
+        local(ckv_hbm, anchor_rows, a1_r)
 
     if hpg is not None:
         @pl.when(pg != hpg)
@@ -184,7 +203,7 @@
             send(anchor_rows, anchor_rows, a2_s, a2_r, target)
 
     pl.semaphore_wait(zs.at[0], 2)
-    near_signal(1)
+    near_signal(zs, 1, z_near)
 
     drain(half_blocks, km_r)
 
@@ -208,9 +227,8 @@
     po[...] = (num / tot).astype(jnp.bfloat16)
     lse = top * COEF + jnp.log(tot) * LOG2E
     lse_row = jnp.sum(jnp.where(col == row, lse, 0.0), axis=0, keepdims=True)
-    lse_tile = jnp.broadcast_to(lse_row, (8, BLK))
-    lsend[...] = lse_tile
-    lbuf[y] = lse_tile
+    lsend[...] = lse_row
+    lbuf[y] = lse_row
     for h2, target in column:
         send(lsend, lbuf.at[y], l_s, l_r, target)
         send(po.at[pl.ds(pl.multiple_of(HALF * h2, HALF), HALF), :], pbuf.at[y], p_s, p_r, target)
@@ -227,11 +245,11 @@
     load_q.wait()
     load_own.wait()
     pl.semaphore_wait(zs.at[1], 2)
-    near_signal(2)
+    near_signal(zs, 2, z_near)
 
     drain(lbuf.at[pl.ds(0, NY - 1)], l_r)
     drain(pbuf.at[pl.ds(0, NY - 1)], p_r)
-    lses = [lbuf[i][0:1, :] for i in range(NY)]
+    lses = [lbuf[i] for i in range(NY)]
     best = functools.reduce(jnp.maximum, lses)
     fac = [jnp.exp2(v - best) for v in lses]
     inv = 1.0 / functools.reduce(jnp.add, fac)
@@ -329,7 +347,7 @@
             jax.ShapeDtypeStruct((BLK, HEADS * DH), bf),
             jax.ShapeDtypeStruct((BLK // NZ, DH), bf),
         ),
-        in_specs=[smem, smem] + [any_spec] * 5,
+        in_specs=[smem] * 2 + [any_spec] * 5,
         out_specs=(any_spec, pl.BlockSpec(memory_space=pltpu.VMEM)),
         scratch_shapes=[
             pltpu.VMEM((BLK, HEADS * DH), bf),
@@ -342,14 +360,15 @@
             pltpu.VMEM((8 if hx is None else 2, 32, DH), bf),
             pltpu.VMEM((32, DH), bf),
             pltpu.VMEM((BLK, DH), bf),
-            pltpu.VMEM((8, BLK), jnp.float32),
+            pltpu.VMEM((1, BLK), jnp.float32),
             pltpu.VMEM((NY, HALF, DH), bf),
-            pltpu.VMEM((NY, 8, BLK), jnp.float32),
+            pltpu.VMEM((NY, 1, BLK), jnp.float32),
             pltpu.VMEM((BLK, HEADS * DH), bf),
             pltpu.VMEM((BLK, DH), bf),
             pltpu.VMEM((NZ, 16, DH), bf),
             pltpu.VMEM((BLK, HEADS * DH), bf),
             dma((3,)),
+            pltpu.SemaphoreType.REGULAR((3,)),
             pltpu.SemaphoreType.REGULAR((3,)),
         ] + [dma] * 27,
         compiler_params=pltpu.CompilerParams(

time: 45.6 us -> 43.9 us (0.963)
  Pallas kernels: 42.3 us -> 40.5 us
    pallas_call x1, Pallas kernels: 42.3 us -> 40.5 us  [call(): pl.pallas_call(functools.partial(kernel, hx, hpg), out_shape=(jax.ShapeDt...]
where the time goes in v3:
time: 43.9 us; the launch traced here: 43.8 us
  Pallas kernels  40.5 us (92%)
  between operations  1.93 us (4%)
  local copies, waits for them, and re-layouts  1.3 us (3%)
    pallas_call x1, Pallas kernels, call(): pl.pallas_call(functools.partial(kernel, hx, hpg), out_shape=(jax.ShapeDt...  40.5 us
    unnamed x2, local copies, waits for them, and re-layouts  1.3 us

profile of v3, /device:TPU:1, one launch (start us, length us, event | category | flops | bytes accessed | tf_op | source)
XLA Modules:
  0.0 43.8 jit_solution(8623800544327325593)
XLA Ops:
  1.9 40.5 %star_attention.1 = (bf16[128,1024]{1,0:T(8,128)(2,1)S(1)}, bf16[16,128]{1,0:T(8,128)(2,1)S(1)}) custom-call(s32[1]{0:T(128)S(6)} %copy.11.len_ref, s32[1]{0:T(128)S(6)} %copy.12.host_ref, bf16[128,1024]{1,0:T(8,128)(2,1)} %cq_hbm.1, bf16[2,128,128]{2,1,0:T(8,128)(2,1)} %ckv_hbm.1, bf16[1,128,1024]{2,1,0:T(8,128)(2,1)} %qq_hbm.1, ...), custom_call_target="tpu_custom_call" | custom-call | tf_op jit(solution)/shard_map/star_attention/pallas_call | solution.py:344
  42.5 0.7 %copy.13 = bf16[128,1024]{1,0:T(8,128)(2,1)} copy(bf16[128,1024]{1,0:T(8,128)(2,1)S(1)} %get-tuple-element.4) | data formatting | bytes 524288
  43.2 0.6 %copy.14 = bf16[16,128]{1,0:T(8,128)(2,1)} copy(bf16[16,128]{1,0:T(8,128)(2,1)S(1)} %get-tuple-element.5) | data formatting | bytes 8192

commit v4 on v3

--- a/solution.py
+++ b/solution.py
@@ -196,12 +196,6 @@
 
     is_source = (x == 0) & (c == 0)
 
-    @pl.when(is_source)
-    def _():
-        drain(anchor_rows, a1_r)
-        for target in same_core:
-            send(anchor_rows, anchor_rows, a2_s, a2_r, target)
-
     pl.semaphore_wait(zs.at[0], 2)
     near_signal(zs, 1, z_near)
 
@@ -229,18 +223,19 @@
     lse_row = jnp.sum(jnp.where(col == row, lse, 0.0), axis=0, keepdims=True)
     lsend[...] = lse_row
     lbuf[y] = lse_row
-    for h2, target in column:
-        send(lsend, lbuf.at[y], l_s, l_r, target)
-        send(po.at[pl.ds(pl.multiple_of(HALF * h2, HALF), HALF), :], pbuf.at[y], p_s, p_r, target)
+    for y2 in (0, 1, 7, 2, 6, 3, 5, 4):
+        @pl.when(y2 != y)
+        def _(y2=y2):
+            send(lsend, lbuf.at[y], l_s, l_r, at(x, y2, c, z))
+            send(po.at[pl.ds(HALF * (y2 % 2), HALF), :], pbuf.at[y], p_s, p_r, at(x, y2, c, z))
+
     pbuf[y] = po[pl.ds(pl.multiple_of(HALF * yp, HALF), HALF), :]
 
-    @pl.when(c == 0)
-    def _():
-        @pl.when(jnp.logical_not(is_source))
-        def _():
-            drain(anchor_rows, a2_r)
-
-        send(anchor_rows, anchor_rows, am_s, am_r, mate)
+    @pl.when(is_source)
+    def _():
+        drain(anchor_rows, a1_r)
+        for target in same_core:
+            send(anchor_rows, anchor_rows, a2_s, a2_r, target)
 
     load_q.wait()
     load_own.wait()
@@ -263,12 +258,19 @@
     attn = jnp.where(hrow < length, attn, 0.0).astype(jnp.bfloat16)
     mine = abuf.at[pl.ds(pl.multiple_of(HALF * yp, HALF), HALF), pl.ds(pl.multiple_of(DH * head, DH), DH)]
     mine[...] = attn
-    for dp, dc, x2, yp2, c2, target in group:
-        send(mine, mine, g_s, g_r, target)
-
-    @pl.when(c == 1)
-    def _():
-        drain(anchor_rows, am_r)
+    for x2, yp2, c2 in [(x2, yp2, c2) for x2 in (0, 1, 3, 2) for yp2 in range(2) for c2 in (1, 0)]:
+        @pl.when((x2 != x) | (yp2 != yp) | (c2 != c))
+        def _(x2=x2, yp2=yp2, c2=c2):
+            send(mine, mine, g_s, g_r, at(x2, pg * 2 + yp2, c2, z))
+
+
+    @pl.when(c == 0)
+    def _():
+        @pl.when(jnp.logical_not(is_source))
+        def _():
+            drain(anchor_rows, a2_r)
+
+        send(anchor_rows, anchor_rows, am_s, am_r, mate)
 
     ccol = lax.broadcasted_iota(jnp.int32, (BLK, 2 * BLK), 1)
     crow = lax.broadcasted_iota(jnp.int32, (BLK, 2 * BLK), 0)
@@ -285,17 +287,22 @@
             nm = jnp.dot(pw.astype(jnp.bfloat16), akv[1], preferred_element_type=jnp.float32)
             cout[:, h * DH:(h + 1) * DH] = (nm / tl).astype(jnp.bfloat16)
 
-    context_heads(0, 4)
-
     load_w.wait()
     pl.semaphore_wait(zs.at[2], 2)
     drain(halves(15), g_r)
     zsrc[...] = jnp.dot(abuf[...], w[...], preferred_element_type=jnp.float32).astype(jnp.bfloat16)
-    for z2, target in heads_z:
-        send(zsrc.at[pl.ds(pl.multiple_of(16 * z2, 16), 16), :], zbuf.at[z], z_s, z_r, target)
+    for z2 in range(NZ):
+        @pl.when(z2 != z)
+        def _(z2=z2):
+            send(zsrc.at[pl.ds(16 * z2, 16), :], zbuf.at[z], z_s, z_r, at(x, y, c, z2))
+
     zbuf[z] = zsrc[pl.ds(pl.multiple_of(16 * z, 16), 16), :]
 
-    context_heads(4, 8)
+    @pl.when(c == 1)
+    def _():
+        drain(anchor_rows, am_r)
+
+    context_heads(0, 8)
     store_c = local(cout, cout_hbm, osem)
 
     @when(sender)

time: 43.9 us -> 43 us (0.979)
  Pallas kernels: 40.5 us -> 39.7 us
    pallas_call x1, Pallas kernels: 40.5 us -> 39.7 us  [call(): pl.pallas_call(functools.partial(kernel, hx, hpg), out_shape=(jax.ShapeDt...]
where the time goes in v4:
time: 43 us; the launch traced here: 42.9 us
  Pallas kernels  39.7 us (92%)
  between operations  1.93 us (4%)
  local copies, waits for them, and re-layouts  1.3 us (3%)
    pallas_call x1, Pallas kernels, call(): pl.pallas_call(functools.partial(kernel, hx, hpg), out_shape=(jax.ShapeDt...  39.7 us
    unnamed x2, local copies, waits for them, and re-layouts  1.3 us

profile of v4, /device:TPU:1, one launch (start us, length us, event | category | flops | bytes accessed | tf_op | source)
XLA Modules:
  0.0 42.9 jit_solution(5601675750749416933)
XLA Ops:
  1.9 39.7 %star_attention.1 = (bf16[128,1024]{1,0:T(8,128)(2,1)S(1)}, bf16[16,128]{1,0:T(8,128)(2,1)S(1)}) custom-call(s32[1]{0:T(128)S(6)} %copy.11.len_ref, s32[1]{0:T(128)S(6)} %copy.12.host_ref, bf16[128,1024]{1,0:T(8,128)(2,1)} %cq_hbm.1, bf16[2,128,128]{2,1,0:T(8,128)(2,1)} %ckv_hbm.1, bf16[1,128,1024]{2,1,0:T(8,128)(2,1)} %qq_hbm.1, ...), custom_call_target="tpu_custom_call" | custom-call | tf_op jit(solution)/shard_map/star_attention/pallas_call | solution.py:351
  41.6 0.7 %copy.13 = bf16[128,1024]{1,0:T(8,128)(2,1)} copy(bf16[128,1024]{1,0:T(8,128)(2,1)S(1)} %get-tuple-element.4) | data formatting | bytes 524288
  42.3 0.6 %copy.14 = bf16[16,128]{1,0:T(8,128)(2,1)} copy(bf16[16,128]{1,0:T(8,128)(2,1)S(1)} %get-tuple-element.5) | data formatting | bytes 8192
